TPU v7x, 32 devices: a whole 2x2x4 slice. The times are simulated.
32 devices in a mesh: group: 2 (over x), lane: 16 (over z, y, core).
Axes of the slice: x: 2, y: 2, z: 4, core: 2. Of those that a mesh axis runs over, the one named last changes fastest.
Arguments:
- queries: bfloat16 [8, 768], replicated, may hold values from -6 to 6
- hyper_weight: bfloat16 [768, 589824], P(None, ('group', 'lane')), may hold values from -0.0078125 to 0.0078125
- hyper_bias: bfloat16 [768, 768], P(None, ('group', 'lane')), may hold values from -0.21875 to 0.21875
- documents: bfloat16 [16384, 768], P(('group', 'lane')), may hold values from -6 to 6
- teacher: bfloat16 [16384, 8], P(('group', 'lane')), may hold values from 8 to 24
Outputs:
- doc_grad: bfloat16 [16384, 768], P(('group', 'lane'))
- weight_grad: bfloat16 [768, 589824], P(None, ('group', 'lane'))
- bias_grad: bfloat16 [768, 768], P(None, ('group', 'lane'))
All inputs are finite; a program needn't handle non-finite values.
Results may differ from a plain program's by a relative error of at most 0.024.
The roundings to bfloat16 on the way count: a program that leaves them out, or rounds other values in their place, can miss the bound.
Values may be sent and summed in bfloat16 or wider, within the bound.
A program may use at most 192 MiB of HBM per device.

v0:
```python
import jax
import jax.numpy as jnp
from jax import lax
from jax.sharding import PartitionSpec as P


def shards(queries, hyper_weight, hyper_bias, documents, teacher):
    features = queries.shape[1]
    group_count = lax.axis_size("group")
    lane_count = lax.axis_size("lane")
    per_group = queries.shape[0] // group_count
    layer_rows = hyper_weight.shape[1] // features
    pool_scale = features ** (-0.5)
    generated = (
        jnp.dot(queries, hyper_weight, preferred_element_type=jnp.float32)
        .astype(jnp.bfloat16)
        .reshape(-1, layer_rows, features)
    )
    bias_part = jnp.dot(queries, hyper_bias, preferred_element_type=jnp.float32).astype(
        jnp.bfloat16
    )
    doc_rows, targets = (
        lax.all_gather(documents, "group", axis=0, tiled=True),
        lax.all_gather(teacher, "group", axis=0, tiled=True),
    )
    first_query = lax.axis_index("group") * per_group
    targets = lax.dynamic_slice_in_dim(targets, first_query, per_group, 1).astype(jnp.float32)
    pieces, bias_pieces = (
        lax.all_to_all(generated, "group", split_axis=0, concat_axis=1, tiled=True),
        lax.all_to_all(bias_part, "group", split_axis=0, concat_axis=1, tiled=True),
    )
    pieces, bias_pieces = (
        lax.all_gather(pieces, "lane", axis=1, tiled=True),
        lax.all_gather(bias_pieces, "lane", axis=1, tiled=True),
    )
    layers = (
        pieces.reshape(per_group, lane_count, group_count, layer_rows, features)
        .transpose(0, 2, 1, 3, 4)
        .reshape(per_group, features, features)
    )
    biases = (
        bias_pieces.reshape(per_group, lane_count, group_count, layer_rows)
        .transpose(0, 2, 1, 3)
        .reshape(per_group, features)
    )
    layer_list = []
    bias_list = []
    doc_total = None
    for number in range(per_group):
        preact = jnp.dot(doc_rows, layers[number], preferred_element_type=jnp.float32) + biases[
            number
        ].astype(jnp.float32)
        scores = jnp.sum(jnp.maximum(preact, 0.0), axis=1) * pool_scale
        errors = scores - targets[:, number]
        back_pre = jnp.where(preact > 0, errors[:, None] * pool_scale, 0.0).astype(jnp.bfloat16)
        layer_list.append(
            lax.dot_general(
                doc_rows, back_pre, (((0,), (0,)), ((), ())), preferred_element_type=jnp.float32
            )
        )
        bias_list.append(jnp.sum(back_pre.astype(jnp.float32), axis=0))
        doc_term = lax.dot_general(
            back_pre, layers[number], (((1,), (1,)), ((), ())), preferred_element_type=jnp.float32
        )
        doc_total = doc_term if doc_total is None else doc_total + doc_term
    layer_grads = jnp.stack(layer_list)
    bias_grads = jnp.stack(bias_list)
    ordered = (
        layer_grads.reshape(per_group, group_count, lane_count, layer_rows, features)
        .transpose(0, 2, 1, 3, 4)
        .reshape(per_group, features, features)
    )
    bias_ordered = (
        bias_grads.reshape(per_group, group_count, lane_count, layer_rows)
        .transpose(0, 2, 1, 3)
        .reshape(per_group, features)
    )
    grads, bias_sums = (
        lax.psum_scatter(ordered, "lane", scatter_dimension=1, tiled=True),
        lax.psum_scatter(bias_ordered, "lane", scatter_dimension=1, tiled=True),
    )
    grads, bias_sums = (
        lax.all_to_all(
            grads.astype(jnp.bfloat16), "group", split_axis=1, concat_axis=0, tiled=True
        ).astype(grads.dtype),
        lax.all_to_all(
            bias_sums.astype(jnp.bfloat16), "group", split_axis=1, concat_axis=0, tiled=True
        ).astype(bias_sums.dtype),
    )
    gen_grad = grads.astype(jnp.bfloat16).reshape(-1, layer_rows * features)
    gen_bias_grad = bias_sums.astype(jnp.bfloat16)
    weight_grad = lax.dot_general(
        queries, gen_grad, (((0,), (0,)), ((), ())), preferred_element_type=jnp.float32
    ).astype(jnp.bfloat16)
    bias_grad = lax.dot_general(
        queries, gen_bias_grad, (((0,), (0,)), ((), ())), preferred_element_type=jnp.float32
    ).astype(jnp.bfloat16)
    doc_grad = lax.psum_scatter(
        doc_total.astype(jnp.bfloat16), "group", scatter_dimension=0, tiled=True
    )
    return (doc_grad, weight_grad, bias_grad)


def solution(mesh):
    placed = (
        P(),
        P(None, ("group", "lane")),
        P(None, ("group", "lane")),
        P(("group", "lane"), None),
        P(("group", "lane"), None),
    )
    return jax.shard_map(
        shards,
        mesh=mesh,
        in_specs=placed,
        out_specs=(
            P(("group", "lane"), None),
            P(None, ("group", "lane")),
            P(None, ("group", "lane")),
        ),
        check_vma=False,
    )
```

profile of v0, /device:TPU:0, one launch (start us, length us, event | category | flops | bytes accessed | tf_op | source)
XLA Modules:
  0.0 377.2 jit_solution(15141647383459870396)
XLA Ops:
  7.2 0.0 all-gather.4.cloned.1.call-start
  7.2 12.8 %convolution_convert_fusion.1 = bf16[8,18432]{1,0:T(8,128)(2,1)S(1)} fusion(bf16[8,768]{1,0:T(8,128)(2,1)} %param.5, bf16[768,18432]{1,0:T(8,128)(2,1)} %param.6), kind=kOutput, calls=%fused_computation.2 | convolution fusion | flops 226639872 | bytes 28618752 | tf_op jit(solution)/shard_map/dot_general | solution.py:15
  20.1 0.1 copy.34
  20.1 9.5 %all_to_all.71 = bf16[8,24,768]{2,1,0:T(8,128)(2,1)S(1)} all-to-all(bf16[8,24,768]{2,1,0:T(8,128)(2,1)S(1)} %copy.34), channel_id=1, replica_groups=mesh['group'=2,'lane'=16] {'group'}, dimensions={0} | all-to-all | bytes 589824 | tf_op jit(solution)/shard_map/all_to_all | solution.py:29
  29.6 0.7 copy.35
  30.4 0.0 all-gather.4.cloned.1.call-update
  30.4 0.0 all-gather.6.cloned.1.call-start
  30.4 0.7 all-gather.6.cloned.1.call-update
  31.2 0.7 convolution_convert_fusion.3
  31.9 3.2 all-to-all-start.1
  35.1 0.0 reduce-scatter.10.cloned.1.call-start
  35.2 4.4 %all_gather.15 = bf16[1024,8]{0,1:T(8,128)(2,1)S(1)} all-gather(bf16[512,8]{0,1:T(8,128)(2,1)S(1)} %copy-done.13), channel_id=1, replica_groups=mesh['group'=2,'lane'=16] {'group'}, dimensions={0}, use_global_device_ids=true | all-gather | bytes 24576 | tf_op jit(solution)/shard_map/all_gather | solution.py:24
  39.6 0.1 all_to_all.59
  39.7 21.9 %all-gather = bf16[16,48,4]{1,2,0:T(4,128)(2,1)S(1)} all-gather(bf16[1,48,4]{1,2,0:T(4,128)(2,1)S(1)} %bitcast.140), channel_id=1, replica_groups=mesh['group'=2,'lane'=16] {'lane'}, dimensions={0}, use_global_device_ids=true | all-gather | bytes 6528 | tf_op jit(solution)/shard_map/all_gather | solution.py:34
  61.6 0.1 reshape.146
  61.7 0.1 reshape.137
  61.8 0.1 reshape.144
  61.9 0.1 reshape.143
  62.0 0.1 reshape.142
  62.1 0.1 reshape.141
  62.2 22.2 %all-gather.4.cloned.1.call-done = bf16[4,768,768]{2,1,0:T(8,128)(2,1)} async-done(((bf16[4,48,768]{2,1,0:T(8,128)(2,1)}), bf16[4,768,768]{2,1,0:T(8,128)(2,1)}) %all-gather.4.cloned.1.call-update) | async-done | bytes 4718608 | tf_op jit(solution)/shard_map/all_gather | solution.py:33
  84.3 2.7 copy.57
  87.0 1.8 fusion.6
  88.8 22.9 %all-gather.6.cloned.1.call-done = bf16[1024,768]{1,0:T(8,128)(2,1)} async-done(((bf16[512,768]{1,0:T(8,128)(2,1)}), bf16[1024,768]{1,0:T(8,128)(2,1)}) %all-gather.6.cloned.1.call-update) | async-done | bytes 1572880 | tf_op jit(solution)/shard_map/all_gather | solution.py:23
  111.7 3.2 maximum_reduce_fusion
  114.9 3.2 maximum_reduce_fusion.1
  118.1 3.3 maximum_reduce_fusion.2
  121.4 3.2 maximum_reduce_fusion.3
  124.7 0.6 convert_reduce_fusion
  125.3 0.1 stack.38
  125.4 3.6 convert_reduce_fusion.1
  128.9 0.1 stack.37
  129.0 3.7 convert_reduce_fusion.2
  132.7 0.1 stack.36
  132.7 3.6 convert_reduce_fusion.3
  136.3 0.1 stack.35
  136.4 1.0 copy.52
  137.5 0.3 reduce-scatter.8.cloned.1.call-start
  137.7 3.1 fusion.13
  140.9 1.5 fusion.12
  142.4 1.5 fusion.11
  143.9 1.5 fusion.10
  145.5 0.8 pad_maximum_fusion
  146.2 5.1 %copy.49 = f32[4,2,16,24,768]{4,3,1,2,0:T(8,128)} copy(f32[4,2,16,24,768]{4,3,2,1,0:T(8,128)S(1)} %pad_maximum_fusion) | data formatting | bytes 18874368 | tf_op jit(solution)/shard_map/stack | solution.py:66
  151.4 0.3 reduce-scatter.6.cloned.1.call-start
  151.7 3.4 fusion.9
  155.1 1.4 fusion.7
  156.6 0.3 copy-done.8
  156.9 1.4 fusion.8
  158.3 2.8 add_convert_fusion
  161.1 32.1 %reduce-scatter.10.cloned.1.call-done = f32[48,4]{1,0:T(8,128)} async-done(((f32[768,4]{1,0:T(8,128)}), f32[48,4]{1,0:T(8,128)}) %reduce-scatter.10.cloned.1.call-update) | async-done | bytes 784
  193.2 0.8 copy.51
  194.0 0.1 all_to_all.63
  194.1 0.6 copy.47
  194.7 3.2 all-to-all-start.3
  197.9 110.8 %reduce-scatter.8.cloned.1.call-done = f32[4,48,768]{2,1,0:T(8,128)} async-done(((f32[4,768,768]{2,1,0:T(8,128)}), f32[4,48,768]{2,1,0:T(8,128)}) %reduce-scatter.8.cloned.1.call-update) | async-done | bytes 589840 | tf_op jit(solution)/shard_map/reduce_scatter | solution.py:79
  308.7 1.1 convert_element_type.126
  309.8 0.9 copy.44
  310.6 3.5 all-to-all-start.2
  314.1 0.8 fusion.1
  314.9 6.4 %all-to-all-done.2 = bf16[4,48,768]{2,0,1:T(4,128)(2,1)S(1)} async-done(((bf16[4,48,768]{2,0,1:T(4,128)(2,1)}), bf16[4,48,768]{2,0,1:T(4,128)(2,1)S(1)}, u32[]{:S(2)}, u32[]{:S(2)}) %all-to-all-start.2) | async-done | bytes 294944 | tf_op jit(solution)/shard_map/all_to_all | solution.py:83
  321.4 0.1 copy.54
  321.4 12.7 %fusion = bf16[768,18432]{0,1:T(8,128)(2,1)} fusion(bf16[8,18432]{1,0:T(8,128)(2,1)S(1)} %bitcast.114, bf16[8,768]{1,0:T(8,128)(2,1)S(1)} %copy-done.12), kind=kOutput, calls=%fused_computation.1 | convolution fusion | flops 240648192 | bytes 28618752 | tf_op jit(solution)/shard_map/dot_general | solution.py:92
  334.1 36.6 %copy.48 = bf16[768,18432]{1,0:T(8,128)(2,1)} copy(bf16[768,18432]{0,1:T(8,128)(2,1)} %fusion) | data formatting | bytes 56623104
  (49 shorter events, 0.2 us)
Async XLA Ops:
  7.2 24.0 %copy-start = (bf16[768,24]{0,1:T(8,128)(2,1)S(1)}, bf16[768,24]{0,1:T(8,128)(2,1)}, u32[]{:S(2)}) copy-start(bf16[768,24]{0,1:T(8,128)(2,1)} %param.7) | copy-start | bytes 110596
  7.2 77.1 %all-gather.4.cloned.1.call-start = ((), (), s32[]{:S(2)}) async-start(), calls=%async_computation.7 | async-start | bytes 5013504 | tf_op jit(solution)/shard_map/all_gather | solution.py:33
  20.1 11.1 %copy-start.12 = (bf16[8,768]{1,0:T(8,128)(2,1)S(1)}, bf16[8,768]{1,0:T(8,128)(2,1)}, u32[]{:S(2)}) copy-start(bf16[8,768]{1,0:T(8,128)(2,1)} %param.5) | copy-start | bytes 36868
  20.1 15.1 %copy-start.13 = (bf16[512,8]{0,1:T(8,128)(2,1)S(1)}, bf16[512,8]{0,1:T(8,128)(2,1)}, u32[]{:S(2)}) copy-start(bf16[512,8]{0,1:T(8,128)(2,1)} %param.9) | copy-start | bytes 24580
  30.4 81.3 %all-gather.6.cloned.1.call-start = ((), (), s32[]{:S(2)}) async-start(), calls=%async_computation.8 | async-start | bytes 2359296 | tf_op jit(solution)/shard_map/all_gather | solution.py:23
  31.9 7.7 %all-to-all-start.1 = ((bf16[2,4,24]{2,1,0:T(4,128)(2,1)}), bf16[2,4,24]{2,1,0:T(4,128)(2,1)S(1)}, u32[]{:S(2)}, u32[]{:S(2)}) async-start(bf16[2,4,24]{2,1,0:T(4,128)(2,1)} %bitcast.7), calls=%async_computation.1 | async-start | bytes 4096 | tf_op jit(solution)/shard_map/all_to_all | solution.py:30
  35.1 158.1 %reduce-scatter.10.cloned.1.call-start = ((), (), s32[]{:S(2)}) async-start(), calls=%async_computation.11 | async-start | bytes 417792
  88.8 29.4 %copy-start.7 = (bf16[1,2,16,24,768]{4,3,2,1,0:T(8,128)(2,1)}, bf16[1,2,16,24,768]{4,3,2,1,0:T(8,128)(2,1)S(1)}, u32[]{:S(2)}) copy-start(bf16[1,2,16,24,768]{4,3,2,1,0:T(8,128)(2,1)S(1)} %get-tuple-element.25) | copy-start | bytes 3538948
  111.7 3.2 copy-start.11
  111.7 3.2 copy-start.14
  118.1 3.3 copy-start.9
  137.5 171.2 %reduce-scatter.8.cloned.1.call-start = ((), (), s32[]{:S(2)}) async-start(), calls=%async_computation.10 | async-start | bytes 10027008 | tf_op jit(solution)/shard_map/reduce_scatter | solution.py:79
  137.7 3.1 copy-start.2
  137.7 3.1 copy-start.15
  140.8 1.5 copy-start.3
  142.4 1.5 copy-start.5
  151.4 219.3 %reduce-scatter.6.cloned.1.call-start = ((), (), s32[]{:S(2)}) async-start(), calls=%async_computation.9 | async-start | bytes 2359296 | tf_op jit(solution)/shard_map/reduce_scatter | solution.py:98
  151.7 3.4 copy-start.6
  151.7 3.4 copy-start.10
  155.1 1.5 copy-start.4
  155.1 1.7 copy-start.8
  194.7 115.9 %all-to-all-start.3 = ((bf16[4,2,24]{2,0,1:T(4,128)(2,1)}), bf16[4,2,24]{2,0,1:T(4,128)(2,1)S(1)}, u32[]{:S(2)}, u32[]{:S(2)}) async-start(bf16[4,2,24]{2,0,1:T(4,128)(2,1)} %copy.47), calls=%async_computation.5 | async-start | bytes 4096 | tf_op jit(solution)/shard_map/all_to_all | solution.py:86
  310.6 10.7 %all-to-all-start.2 = ((bf16[4,48,768]{2,0,1:T(4,128)(2,1)}), bf16[4,48,768]{2,0,1:T(4,128)(2,1)S(1)}, u32[]{:S(2)}, u32[]{:S(2)}) async-start(bf16[4,48,768]{2,0,1:T(4,128)(2,1)} %copy.44), calls=%async_computation.4 | async-start | bytes 589824 | tf_op jit(solution)/shard_map/all_to_all | solution.py:83
  334.1 36.6 %copy-start.1 = (bf16[768,24]{0,1:T(8,128)(2,1)S(1)}, bf16[768,24]{0,1:T(8,128)(2,1)}, u32[]{:S(2)}) copy-start(bf16[768,24]{0,1:T(8,128)(2,1)} %param.7) | copy-start | bytes 110596
Sparse Core Ops, SparseCore 0:
  30.5 53.7 all-gather.3
  85.9 25.7 all-gather.5
  137.6 55.5 reduce-scatter.9
  198.3 110.3 reduce-scatter.7
  311.3 26.5 reduce-scatter.5
where the time goes:
time: 379 us; the launch traced here: 377 us
  waiting for transfers between devices  195 us (51%)
  matrix products  56.6 us (15%)
  local copies, waits for them, and re-layouts  51.7 us (14%)
  blocking collectives  35.8 us (9%)
  between operations  14.2 us (4%)
  other arithmetic  13.3 us (4%)
  starting transfers between devices  10.6 us (3%)
    reduce_scatter x1, waiting for transfers between devices, shards(): lax.psum_scatter(ordered, 'lane', scatter_dimension=1, tiled=True)  111 us
    unnamed x37, local copies, waits for them, and re-layouts  38.9 us
    unnamed x6, waiting for transfers between devices  32.8 us
    all_gather x1, waiting for transfers between devices, shards(): lax.all_gather(documents, 'group', axis=0, tiled=True)  22.9 us
    all_gather x1, waiting for transfers between devices, shards(): lax.all_gather(pieces, 'lane', axis=1, tiled=True)  22.2 us
    all_gather x1, blocking collectives, shards(): lax.all_gather(bias_pieces, 'lane', axis=1, tiled=True)  21.9 us
    dot_general x4, matrix products, shards(): jnp.dot(doc_rows, layers[number], preferred_element_type=jnp.float32)  12.9 us
    dot_general x1, matrix products, shards(): jnp.dot(queries, hyper_weight, preferred_element_type=jnp.float32)  12.8 us
  transfers between devices with their start and end apart: 8, of which 5 were waited for; matrix products, arithmetic and copies ran while one was open for 22% of the time, Pallas kernels for 0%

commit v1 on v0

--- a/solution.py
+++ b/solution.py
@@ -1,7 +1,374 @@
+import functools
+
 import jax
 import jax.numpy as jnp
 from jax import lax
+from jax.experimental import pallas as pl
+from jax.experimental.pallas import tpu as pltpu
 from jax.sharding import PartitionSpec as P
+
+MESH = pl.DeviceIdType.MESH
+MIB = 1024 * 1024
+
+
+def window_kernel(
+    depth,
+    per_group,
+    layer_rows,
+    scale,
+    docs_ref,
+    docs_t_ref,
+    layers_ref,
+    bias_ref,
+    target_ref,
+    doc_out,
+    grad_out,
+    bias_out,
+    back_ref,
+    doc_acc,
+    sums,
+    send1,
+    recv1,
+    send2,
+    recv2,
+    send3,
+    recv3,
+    final,
+    send4,
+    recv4,
+    doc_send,
+    doc_recv,
+    bias_send,
+    bias_recv,
+    s1,
+    r1,
+    s2,
+    r2,
+    s3,
+    r3,
+    sb,
+    rb,
+    sx,
+    rx,
+):
+    group = lax.axis_index("group")
+    lane = lax.axis_index("lane")
+    core = lax.rem(lane, 2)
+    y = lax.rem(lane // 2, 2)
+    z = lane // 4
+    chunk = 2 * layer_rows
+    features = layers_ref.shape[1]
+    doc_rows = docs_ref.shape[0]
+    own_docs = doc_rows // 2
+    to_core = (group, lane + 1 - 2 * core)
+    to_y = (group, lane + 2 - 4 * y)
+    to_x = (1 - group, lane)
+
+    def z_peer(step):
+        return lax.rem(z + step, depth)
+
+    def to_z(step):
+        return (group, z_peer(step) * 4 + y * 2 + core)
+
+    peers = [to_core, to_y, to_x] + [to_z(step) for step in range(1, depth)]
+    barrier = pltpu.get_barrier_semaphore()
+    for peer in peers:
+        pl.semaphore_signal(barrier, inc=1, device_id=peer, device_id_type=MESH)
+    pl.semaphore_wait(barrier, len(peers))
+
+    def remote(src, dst, send_sem, recv_sem, peer):
+        return pltpu.make_async_remote_copy(
+            src_ref=src,
+            dst_ref=dst,
+            send_sem=send_sem,
+            recv_sem=recv_sem,
+            device_id=peer,
+            device_id_type=MESH,
+        )
+
+    def copy1(q):
+        return remote(send1.at[q], recv1.at[q], s1.at[q], r1.at[q], to_core)
+
+    def copy2(q):
+        return remote(send2.at[q], recv2.at[q], s2.at[q], r2.at[q], to_y)
+
+    def copy3(q, step):
+        k = step - 1
+        return remote(send3.at[q, k], recv3.at[q, k], s3.at[q, k], r3.at[q, k], to_z(step))
+
+    def bias_copy(k, peer):
+        slot = min(k, 2)
+        return remote(bias_send.at[slot], bias_recv.at[k], sb.at[k], rb.at[k], peer)
+
+    doc_copy = remote(doc_send, doc_recv, sx.at[0], rx.at[0], to_x)
+    grad_copy = remote(send4, recv4, sx.at[1], rx.at[1], to_x)
+    bias_x_copy = remote(bias_send.at[3], bias_recv.at[depth + 1], sx.at[2], rx.at[2], to_x)
+
+    def stage2(q):
+        copy1(q).wait_recv()
+
+        def part(k, carry):
+            mine, theirs = k * 2 + y, k * 2 + 1 - y
+            sums[q, mine, core] = sums[q, mine, core] + recv1[q, mine].astype(jnp.float32)
+            send2[q, k] = (
+                sums[q, theirs, core] + recv1[q, theirs].astype(jnp.float32)
+            ).astype(jnp.bfloat16)
+            return carry
+
+        lax.fori_loop(0, depth, part, 0)
+        copy2(q).start()
+
+    def stage3(q):
+        copy2(q).wait_recv()
+        for step in range(1, depth):
+            to = z_peer(step)
+            send3[q, step - 1] = (
+                sums[q, to * 2 + y, core] + recv2[q, to].astype(jnp.float32)
+            ).astype(jnp.bfloat16)
+            copy3(q, step).start()
+        sums[q, z * 2 + y, core] = sums[q, z * 2 + y, core] + recv2[q, z].astype(jnp.float32)
+
+    def finish(q):
+        total = sums[q, z * 2 + y, core]
+        for step in range(1, depth):
+            copy3(q, step).wait_recv()
+            total = total + recv3[q, step - 1].astype(jnp.float32)
+        final[q] = total.reshape(2, layer_rows, features)
+
+    tile = doc_rows // 4 if doc_rows % 64 == 0 else doc_rows
+    bias_send[0] = jnp.zeros(bias_send.shape[1:], jnp.float32)
+
+    for q in range(per_group):
+
+        def rows_of(c, bias_sum):
+            rows = pl.ds(pl.multiple_of(c * tile, tile), tile)
+            layer = layers_ref[q]
+            preact = (
+                jnp.dot(docs_ref[rows, :], layer, preferred_element_type=jnp.float32)
+                + bias_ref[q : q + 1, :]
+            )
+            scores = jnp.sum(jnp.maximum(preact, 0.0), axis=1, keepdims=True) * scale
+            errors = (scores - target_ref[rows, q : q + 1]) * scale
+            back = jnp.where(preact > 0, errors, 0.0).astype(jnp.bfloat16)
+            back_ref[rows, :] = back
+            term = lax.dot_general(
+                back, layer, (((1,), (1,)), ((), ())), preferred_element_type=jnp.float32
+            )
+            if q == 0:
+                doc_acc[rows, :] = term
+            else:
+                doc_acc[rows, :] = doc_acc[rows, :] + term
+            return bias_sum + jnp.sum(back.astype(jnp.float32), axis=0, keepdims=True)
+
+        bias_send[0, q : q + 1, :] = lax.fori_loop(
+            0, doc_rows // tile, rows_of, jnp.zeros((1, features), jnp.float32)
+        )
+        if q >= 1:
+            stage2(q - 1)
+        if q == per_group - 1:
+            doc_send[...] = doc_acc[own_docs:, :].astype(jnp.bfloat16)
+            doc_copy.start()
+            bias_copy(0, to_core).start()
+
+        def grad_rows(t, carry):
+            size = depth * chunk
+            rows = pl.ds(pl.multiple_of(t * size, size), size)
+            block = jnp.dot(
+                docs_t_ref[rows, :], back_ref[...], preferred_element_type=jnp.float32
+            )
+            first = pl.ds(t * (depth // 2), depth // 2)
+            sums[q, first] = block.reshape(depth // 2, 2, chunk, features)
+            send1[q, first] = sums[q, first, 1 - core].astype(jnp.bfloat16)
+            return carry
+
+        lax.fori_loop(0, 4, grad_rows, 0)
+        copy1(q).start()
+        if q >= 1:
+            stage3(q - 1)
+
+    bias_copy(0, to_core).wait_recv()
+    bias_send[1] = bias_send[0] + bias_recv[0]
+    bias_copy(1, to_y).start()
+    stage2(per_group - 1)
+    bias_copy(1, to_y).wait_recv()
+    bias_send[2] = bias_send[1] + bias_recv[1]
+    for step in range(1, depth):
+        bias_copy(1 + step, to_z(step)).start()
+    for q in range(per_group - 1):
+        finish(q)
+    bias_total = bias_send[2]
+    for step in range(1, depth):
+        bias_copy(1 + step, to_z(step)).wait_recv()
+        bias_total = bias_total + bias_recv[1 + step]
+    bias_send[3] = bias_total
+    bias_x_copy.start()
+    doc_copy.wait_recv()
+    doc_out[...] = (doc_acc[:own_docs, :] + doc_recv[...].astype(jnp.float32)).astype(jnp.bfloat16)
+    stage3(per_group - 1)
+    finish(per_group - 1)
+    send4[...] = final[:, 1 - group].reshape(send4.shape).astype(jnp.bfloat16)
+    grad_copy.start()
+    grad_out[group] = final[:, group].reshape(send4.shape).astype(jnp.bfloat16)
+    bias_out[group] = bias_total
+    bias_x_copy.wait_recv()
+    bias_out[1 - group] = bias_recv[depth + 1]
+    grad_copy.wait_recv()
+    grad_out[1 - group] = recv4[...]
+
+    for q in range(per_group):
+        copy1(q).wait_send()
+        copy2(q).wait_send()
+        for step in range(1, depth):
+            copy3(q, step).wait_send()
+    bias_copy(0, to_core).wait_send()
+    bias_copy(1, to_y).wait_send()
+    for step in range(1, depth):
+        bias_copy(1 + step, to_z(step)).wait_send()
+    doc_copy.wait_send()
+    grad_copy.wait_send()
+    bias_x_copy.wait_send()
+
+
+def window(docs, docs_t, layers, biases, targets, depth, layer_rows, scale):
+    per_group, features, _ = layers.shape
+    doc_rows = docs.shape[0]
+    chunk = 2 * layer_rows
+    pairs = depth * 2
+    bf16, f32 = jnp.bfloat16, jnp.float32
+    vmem = pl.BlockSpec(memory_space=pltpu.VMEM)
+    dma = pltpu.SemaphoreType.DMA
+    flops = 6 * doc_rows * features * features * per_group
+    return pl.pallas_call(
+        functools.partial(window_kernel, depth, per_group, layer_rows, scale),
+        out_shape=(
+            jax.ShapeDtypeStruct((doc_rows // 2, features), bf16),
+            jax.ShapeDtypeStruct((2, per_group * layer_rows, features), bf16),
+            jax.ShapeDtypeStruct((2,) + biases.shape, f32),
+        ),
+        in_specs=[vmem] * 5,
+        out_specs=(vmem, vmem, vmem),
+        scratch_shapes=[
+            pltpu.VMEM((doc_rows, features), bf16),
+            pltpu.VMEM((doc_rows, features), f32),
+            pltpu.VMEM((per_group, pairs, 2, chunk, features), f32),
+            pltpu.VMEM((per_group, pairs, chunk, features), bf16),
+            pltpu.VMEM((per_group, pairs, chunk, features), bf16),
+            pltpu.VMEM((per_group, depth, chunk, features), bf16),
+            pltpu.VMEM((per_group, depth, chunk, features), bf16),
+            pltpu.VMEM((per_group, depth - 1, chunk, features), bf16),
+            pltpu.VMEM((per_group, depth - 1, chunk, features), bf16),
+            pltpu.VMEM((per_group, 2, layer_rows, features), f32),
+            pltpu.VMEM((per_group * layer_rows, features), bf16),
+            pltpu.VMEM((per_group * layer_rows, features), bf16),
+            pltpu.VMEM((doc_rows // 2, features), bf16),
+            pltpu.VMEM((doc_rows // 2, features), bf16),
+            pltpu.VMEM((4,) + biases.shape, f32),
+            pltpu.VMEM((depth + 2,) + biases.shape, f32),
+            dma((per_group,)),
+            dma((per_group,)),
+            dma((per_group,)),
+            dma((per_group,)),
+            dma((per_group, depth - 1)),
+            dma((per_group, depth - 1)),
+            dma((depth + 1,)),
+            dma((depth + 1,)),
+            dma((3,)),
+            dma((3,)),
+        ],
+        compiler_params=pltpu.CompilerParams(
+            collective_id=0, has_side_effects=True, vmem_limit_bytes=56 * MIB
+        ),
+        cost_estimate=pl.CostEstimate(
+            flops=flops, bytes_accessed=8 * MIB, transcendentals=0
+        ),
+        name="window",
+    )(docs, docs_t, layers, biases, targets)
+
+
+def outer_kernel(query_ref, grad_ref, out_ref):
+    out_ref[...] = jnp.dot(
+        query_ref[...], grad_ref[0], preferred_element_type=jnp.float32
+    ).astype(out_ref.dtype)
+
+
+def outer(queries, grads):
+    rows, count, features = grads.shape
+    return pl.pallas_call(
+        outer_kernel,
+        grid=(rows,),
+        out_shape=jax.ShapeDtypeStruct((queries.shape[1], rows * features), jnp.bfloat16),
+        in_specs=[
+            pl.BlockSpec((queries.shape[1], count), lambda r: (0, 0)),
+            pl.BlockSpec((1, count, features), lambda r: (r, 0, 0)),
+        ],
+        out_specs=pl.BlockSpec((queries.shape[1], features), lambda r: (0, r)),
+        compiler_params=pltpu.CompilerParams(vmem_limit_bytes=32 * MIB),
+        name="outer",
+    )(queries.T, grads)
+
+
+def fused_shards(queries, hyper_weight, hyper_bias, documents, teacher):
+    features = queries.shape[1]
+    lane_count = lax.axis_size("lane")
+    per_group = queries.shape[0] // 2
+    layer_rows = hyper_weight.shape[1] // features
+    depth = lane_count // 4
+    scale = features ** (-0.5)
+    group = lax.axis_index("group")
+    swap = [(0, 1), (1, 0)]
+    other_docs = lax.ppermute(documents, "group", swap)
+    other_teacher = lax.ppermute(teacher, "group", swap)
+    generated = jnp.dot(queries, hyper_weight, preferred_element_type=jnp.float32).astype(
+        jnp.bfloat16
+    )
+    bias_part = jnp.dot(queries, hyper_bias, preferred_element_type=jnp.float32).astype(
+        jnp.bfloat16
+    )
+    rows = per_group * layer_rows
+    extra = jnp.pad(
+        bias_part.reshape(2, 1, rows), ((0, 0), (0, 15), (0, features - rows))
+    )
+    packed = jnp.concatenate([generated.reshape(2, rows, features), extra], axis=1)
+    mine = lax.dynamic_index_in_dim(packed, group, 0, keepdims=False)
+    theirs = lax.dynamic_index_in_dim(packed, 1 - group, 0, keepdims=False)
+    got = lax.ppermute(theirs, "group", swap)
+    pieces = jnp.where(group == 0, jnp.stack([mine, got]), jnp.stack([got, mine]))
+    gathered = lax.all_gather(pieces, "lane", axis=0)
+    layers = (
+        gathered[:, :, :rows]
+        .reshape(lane_count, 2, per_group, layer_rows, features)
+        .transpose(2, 1, 0, 3, 4)
+        .reshape(per_group, features, features)
+    )
+    biases = (
+        gathered[:, :, rows, :rows]
+        .reshape(lane_count, 2, per_group, layer_rows)
+        .transpose(2, 1, 0, 3)
+        .reshape(per_group, features)
+        .astype(jnp.float32)
+    )
+    biases = jnp.pad(biases, ((0, -per_group % 8), (0, 0)))
+    docs = jnp.concatenate([documents, other_docs])
+    docs_t = (
+        docs.T.reshape(2, lane_count, layer_rows, docs.shape[0])
+        .transpose(1, 0, 2, 3)
+        .reshape(features, docs.shape[0])
+    )
+    targets = lax.dynamic_slice_in_dim(
+        jnp.concatenate([teacher, other_teacher]), group * per_group, per_group, 1
+    ).astype(jnp.float32)
+    doc_grad, grads, bias_sums = window(
+        docs, docs_t, layers, biases, targets, depth, layer_rows, scale
+    )
+    grads = grads.reshape(2 * per_group, layer_rows, features).transpose(1, 0, 2)
+    weight_grad = outer(queries, grads)
+    first = (group * lane_count + lax.axis_index("lane")) * layer_rows
+    bias_rows = bias_sums[:, :per_group].reshape(2 * per_group, features)
+    gen_bias_grad = lax.dynamic_slice_in_dim(bias_rows, first, layer_rows, 1).astype(jnp.bfloat16)
+    bias_grad = lax.dot_general(
+        queries, gen_bias_grad, (((0,), (0,)), ((), ())), preferred_element_type=jnp.float32
+    ).astype(jnp.bfloat16)
+    return (doc_grad, weight_grad, bias_grad)
 
 
 def shards(queries, hyper_weight, hyper_bias, documents, teacher):
@@ -109,8 +476,17 @@
         P(("group", "lane"), None),
         P(("group", "lane"), None),
     )
+    groups, lanes = mesh.shape["group"], mesh.shape["lane"]
+
+    def body(queries, hyper_weight, hyper_bias, documents, teacher):
+        layer_rows = hyper_weight.shape[1] // queries.shape[1]
+        fits = groups == 2 and lanes in (8, 16) and layer_rows % 8 == 0
+        fits = fits and documents.shape[0] % 32 == 0 and queries.shape[0] % 4 == 0
+        form = fused_shards if fits else shards
+        return form(queries, hyper_weight, hyper_bias, documents, teacher)
+
     return jax.shard_map(
-        shards,
+        body,
         mesh=mesh,
         in_specs=placed,
         out_specs=(

time: 379 us -> 199 us (0.53)
  waiting for transfers between devices: 195 us -> 56.5 us
  Pallas kernels: 0 us -> 92.3 us
  matrix products: 56.6 us -> 14.6 us
  local copies, waits for them, and re-layouts: 51.7 us -> 13.5 us
  blocking collectives: 35.8 us -> 0 us
  other arithmetic: 13.3 us -> 2.25 us
  starting transfers between devices: 10.6 us -> 5.13 us
    reduce_scatter x2 -> x0, waiting for transfers between devices: 111 us -> none  [the longest x1 111 us: shards(): lax.psum_scatter(ordered, 'lane', scatter_dimension=1, tiled=True)]
    pallas_call x0 -> x2, Pallas kernels: none -> 92.3 us  [the longest x1 74.3 us: window(): pl.pallas_call(functools.partial(window_kernel, depth, per_group, layer_r...]
    dot_general x16 -> x3, matrix products: 56.6 us -> 14.6 us  [the longest x1 12.9 us: fused_shards(): jnp.dot(queries, hyper_weight, preferred_element_type=jnp.float32)]
    unnamed x37 -> x18, local copies, waits for them, and re-layouts: 38.9 us -> 2.04 us
    unnamed x6 -> x1, waiting for transfers between devices: 32.8 us -> 0.02 us
    all_gather x2 -> x0, blocking collectives: 26.3 us -> none  [the longest x1 21.9 us: shards(): lax.all_gather(bias_pieces, 'lane', axis=1, tiled=True)]
    ppermute x0 -> x3, waiting for transfers between devices: none -> 21 us  [the longest x1 16.6 us: fused_shards(): other_teacher = lax.ppermute(teacher, 'group', swap)]
    reduce_sum x4 -> x0, other arithmetic: 11.4 us -> none  [shards(): bias_list.append(jnp.sum(back_pre.astype(jnp.float32), axis=0))]
  transfers between devices with their start and end apart: 8 -> 4, of which waited for: 5 -> 3; matrix products, arithmetic and copies ran while one was open for 22% -> 2% of each run, Pallas kernels for 0% -> 0%
where the time goes in v1:
time: 199 us; the launch traced here: 198 us
  Pallas kernels  92.3 us (46%)
  waiting for transfers between devices  56.5 us (28%)
  matrix products  14.6 us (7%)
  between operations  14.2 us (7%)
  local copies, waits for them, and re-layouts  13.5 us (7%)
  starting transfers between devices  5.13 us (3%)
  other arithmetic  2.25 us (1%)
    pallas_call x1, Pallas kernels, window(): pl.pallas_call(functools.partial(window_kernel, depth, per_group, layer_r...  74.3 us
    all_gather x1, waiting for transfers between devices, fused_shards(): gathered = lax.all_gather(pieces, 'lane', axis=0)  35.4 us
    pallas_call x1, Pallas kernels, outer(): pl.pallas_call(outer_kernel, grid=(rows,), out_shape=jax.ShapeDtypeStruct...  17.9 us
    ppermute x1, waiting for transfers between devices, fused_shards(): other_teacher = lax.ppermute(teacher, 'group', swap)  16.6 us
    dot_general x1, matrix products, fused_shards(): jnp.dot(queries, hyper_weight, preferred_element_type=jnp.float32)  12.9 us
    ppermute x1, waiting for transfers between devices, fused_shards(): got = lax.ppermute(theirs, 'group', swap)  4.37 us
  transfers between devices with their start and end apart: 4, of which 3 were waited for; matrix products, arithmetic and copies ran while one was open for 2% of the time, Pallas kernels for 0%

profile of v1, /device:TPU:0, one launch (start us, length us, event | category | flops | bytes accessed | tf_op | source)
XLA Modules:
  0.0 198.5 jit_solution(273285184232843695)
XLA Ops:
  7.2 0.0 copy-start
  7.2 0.0 all-gather.2.cloned.1.call-start
  7.2 0.7 copy-done
  7.9 0.8 convolution_convert_fusion.2
  8.8 0.1 reshape.100
  8.9 0.0 copy-start.3
  8.9 0.0 copy-start.6
  8.9 0.0 copy-start.5
  8.9 12.9 %convolution_convert_fusion = bf16[8,18432]{1,0:T(8,128)(2,1)S(1)} fusion(bf16[8,768]{1,0:T(8,128)(2,1)} %param.5, bf16[768,18432]{1,0:T(8,128)(2,1)} %param.6), kind=kOutput, calls=%fused_computation | convolution fusion | flops 226639872 | bytes 28618752 | tf_op jit(solution)/shard_map/dot_general | solution.py:321
  21.8 0.1 reshape.94
  22.0 3.0 %collective-permute-start.1 = (bf16[112,768]{1,0:T(8,128)(2,1)S(1)}, bf16[112,768]{1,0:T(8,128)(2,1)S(1)}, u32[]{:S(2)}, u32[]{:S(2)}) collective-permute-start(bf16[112,768]{1,0:T(8,128)(2,1)S(1)} %get-tuple-element.10), channel_id=1, source_target_pairs={{0,16},{16,0},{1,17},{17,1},{2,18},{18,2},{3,19},{19,3},{4,20},{20... | collective-permute-start | bytes 516104 | tf_op jit(solution)/shard_map/ppermute | solution.py:334
  25.0 4.4 %collective-permute-done.1 = bf16[112,768]{1,0:T(8,128)(2,1)S(1)} collective-permute-done((bf16[112,768]{1,0:T(8,128)(2,1)S(1)}, bf16[112,768]{1,0:T(8,128)(2,1)S(1)}, u32[]{:S(2)}, u32[]{:S(2)}) %collective-permute-start.1) | collective-permute-done | bytes 172064 | tf_op jit(solution)/shard_map/ppermute | solution.py:334
  29.4 0.8 maximum_select_fusion
  30.1 0.0 all-gather.2.cloned.1.call-update
  30.2 0.0 copy-done.3
  30.2 1.8 collective-permute-start
  32.0 0.0 copy-done.6
  32.0 0.3 collective-permute-start.2
  32.3 0.1 constant_dynamic-update-slice_fusion.1
  32.3 0.0 copy-done.5
  32.3 0.2 copy.30
  32.5 16.6 %collective-permute-done.2 = bf16[512,8]{0,1:T(8,128)(2,1)S(1)} collective-permute-done((bf16[512,8]{0,1:T(8,128)(2,1)S(1)}, bf16[512,8]{0,1:T(8,128)(2,1)S(1)}, u32[]{:S(2)}, u32[]{:S(2)}) %collective-permute-start.2) | collective-permute-done | bytes 8224 | tf_op jit(solution)/shard_map/ppermute | solution.py:320
  49.2 0.2 copy.32
  49.4 0.8 convert_element_type.37.target_ref
  50.2 0.0 collective-permute-done
  50.2 1.2 constant_dynamic-update-slice_fusion.docs_ref
  51.4 0.0 copy-start.2
  51.4 0.9 copy.23
  52.4 1.4 copy.24
  53.8 35.4 %all-gather.2.cloned.1.call-done = bf16[16,2,112,768]{3,2,1,0:T(8,128)(2,1)} async-done(((bf16[1,2,112,768]{3,2,1,0:T(8,128)(2,1)}), bf16[16,2,112,768]{3,2,1,0:T(8,128)(2,1)}) %all-gather.2.cloned.1.call-update) | async-done | bytes 5505040 | tf_op jit(solution)/shard_map/all_gather | solution.py:336
  89.2 0.8 slice.13
  90.1 0.0 slice-start
  90.1 0.0 copy-done.2
  90.1 2.3 %slice-done = bf16[16,2,96,768]{3,2,1,0:T(8,128)(2,1)S(1)} async-done(((bf16[16,2,112,768]{3,2,1,0:T(8,128)(2,1)}), bf16[16,2,96,768]{3,2,1,0:T(8,128)(2,1)S(1)}, s32[]{:S(2)}) %slice-start) | async-done | bytes 4718616 | tf_op jit(solution)/shard_map/slice | solution.py:338
  92.4 2.5 %copy.26 = bf16[4,2,16,24,768]{4,3,2,1,0:T(8,128)(2,1)} copy(bf16[4,2,16,24,768]{4,3,0,1,2:T(8,128)(2,1)S(1)} %bitcast.35) | data formatting | bytes 9437184 | tf_op jit(solution)/shard_map/transpose | solution.py:340
  94.9 0.1 convert_element_type.34
  95.0 0.1 convert_element_type.36
  95.1 0.6 pad_convert_fusion.bias_ref
  95.7 74.3 %window.1 = (bf16[512,768]{1,0:T(8,128)(2,1)}, bf16[2,96,768]{2,1,0:T(8,128)(2,1)}, f32[2,8,768]{2,1,0:T(8,128)}) custom-call(bf16[1024,768]{1,0:T(8,128)(2,1)} %copy-done.2, bf16[768,1024]{1,0:T(8,128)(2,1)} %bitcast.39, bf16[4,768,768]{2,1,0:T(8,128)(2,1)} %bitcast.37, f32[8,768]{1,0:T(8,128)} %pad_convert_fusion.bias_ref, ...), custom_call_target="tpu_custom_call" | custom-call | flops 14495514624 | bytes 8388608 | tf_op jit(solution)/shard_map/window/pallas_call | solution.py:241
  170.1 1.0 copy.34
  171.1 0.8 slice.11
  171.9 0.9 fusion
  172.8 0.0 copy-start.4
  172.8 0.0 copy-start.1
  172.8 17.9 %outer.1 = bf16[768,18432]{1,0:T(8,128)(2,1)} custom-call(bf16[768,8]{1,0:T(8,128)(2,1)S(1)} %bitcast.34, bf16[24,8,768]{2,1,0:T(8,128)(2,1)S(1)} %bitcast.33), custom_call_target="tpu_custom_call" | custom-call | tf_op jit(solution)/shard_map/outer/pallas_call | solution.py:296
  190.8 0.0 copy-done.4
  190.8 0.9 copy.37
  191.6 0.0 copy-done.1
  (6 shorter events, 0.1 us)
Async XLA Ops:
  7.2 0.8 copy-start
  7.2 82.0 %all-gather.2.cloned.1.call-start = ((), (), s32[]{:S(2)}) async-start(), calls=%async_computation | async-start | bytes 5849088 | tf_op jit(solution)/shard_map/all_gather | solution.py:336
  8.9 21.3 %copy-start.3 = (bf16[512,768]{1,0:T(8,128)(2,1)S(1)}, bf16[512,768]{1,0:T(8,128)(2,1)}, u32[]{:S(2)}) copy-start(bf16[512,768]{1,0:T(8,128)(2,1)} %param.8) | copy-start | bytes 2359300
  8.9 23.1 %copy-start.6 = (bf16[512,8]{0,1:T(8,128)(2,1)S(1)}, bf16[512,8]{0,1:T(8,128)(2,1)}, u32[]{:S(2)}) copy-start(bf16[512,8]{0,1:T(8,128)(2,1)} %param.9) | copy-start | bytes 24580
  8.9 23.5 %copy-start.5 = (bf16[8,768]{1,0:T(8,128)(2,1)S(1)}, bf16[8,768]{1,0:T(8,128)(2,1)}, u32[]{:S(2)}) copy-start(bf16[8,768]{1,0:T(8,128)(2,1)} %param.5) | copy-start | bytes 36868
  22.0 7.4 %collective-permute-start.1 = (bf16[112,768]{1,0:T(8,128)(2,1)S(1)}, bf16[112,768]{1,0:T(8,128)(2,1)S(1)}, u32[]{:S(2)}, u32[]{:S(2)}) collective-permute-start(bf16[112,768]{1,0:T(8,128)(2,1)S(1)} %get-tuple-element.10), channel_id=1, source_target_pairs={{0,16},{16,0},{1,17},{17,1},{2,18},{18,2},{3,19},{19,3},{4,20},{20... | collective-permute-start | bytes 516104 | tf_op jit(solution)/shard_map/ppermute | solution.py:334
  30.2 20.0 %collective-permute-start = (bf16[512,768]{1,0:T(8,128)(2,1)S(1)}, bf16[512,768]{1,0:T(8,128)(2,1)}, u32[]{:S(2)}, u32[]{:S(2)}) collective-permute-start(bf16[512,768]{1,0:T(8,128)(2,1)S(1)} %copy-done.3), channel_id=1, source_target_pairs={{0,16},{16,0},{1,17},{17,1},{2,18},{18,2},{3,19},{19,3},{4,20},{20... | collective-permute-start | bytes 2359304 | tf_op jit(solution)/shard_map/ppermute | solution.py:319
  32.0 17.2 %collective-permute-start.2 = (bf16[512,8]{0,1:T(8,128)(2,1)S(1)}, bf16[512,8]{0,1:T(8,128)(2,1)S(1)}, u32[]{:S(2)}, u32[]{:S(2)}) collective-permute-start(bf16[512,8]{0,1:T(8,128)(2,1)S(1)} %copy-done.6), channel_id=1, source_target_pairs={{0,16},{16,0},{1,17},{17,1},{2,18},{18,2},{3,19},{19,3},{4,20},{20... | collective-permute-start | bytes 24584 | tf_op jit(solution)/shard_map/ppermute | solution.py:320
  51.4 38.7 %copy-start.2 = (bf16[1024,768]{1,0:T(8,128)(2,1)}, bf16[1024,768]{1,0:T(8,128)(2,1)S(1)}, u32[]{:S(2)}) copy-start(bf16[1024,768]{1,0:T(8,128)(2,1)S(1)} %constant_dynamic-update-slice_fusion.docs_ref) | copy-start | bytes 4718596
  90.1 2.3 %slice-start = ((bf16[16,2,112,768]{3,2,1,0:T(8,128)(2,1)}), bf16[16,2,96,768]{3,2,1,0:T(8,128)(2,1)S(1)}, s32[]{:S(2)}) async-start(bf16[16,2,112,768]{3,2,1,0:T(8,128)(2,1)} %all-gather.2.cloned.1.call-done), calls=%async_computation.1 | async-start | bytes 9437184 | tf_op jit(solution)/shard_map/slice | solution.py:338
  172.8 17.9 %copy-start.4 = (bf16[512,768]{1,0:T(8,128)(2,1)S(1)}, bf16[512,768]{1,0:T(8,128)(2,1)}, u32[]{:S(2)}) copy-start(bf16[512,768]{1,0:T(8,128)(2,1)} %get-tuple-element.14) | copy-start | bytes 2359300
  172.8 18.8 %copy-start.1 = (bf16[768,24]{0,1:T(8,128)(2,1)S(1)}, bf16[768,24]{0,1:T(8,128)(2,1)}, u32[]{:S(2)}) copy-start(bf16[768,24]{0,1:T(8,128)(2,1)} %param.7) | copy-start | bytes 110596
Sparse Core Ops, SparseCore 0:
  30.3 58.8 all-gather.1
